TPU v7x, 256 devices: a whole 4x4x8 slice. The times are simulated.
256 devices in a mesh: dp: 4 (over z_hi, core), expert: 64 (over y, x, z_lo).
Axes of the slice: x: 4, y: 4, z: 8 (z_hi: 2, z_lo: 4; z = z_hi * 4 + z_lo), core: 2. Of those that a mesh axis runs over, the one named last changes fastest.
Arguments:
- tokens: bfloat16 [32768, 2048], P(('dp', 'expert')), may hold values from -6 to 6
- routes: int32 [32768, 8], P(('dp', 'expert')), may hold values from 0 to 63, all different within a row; in each aligned block of 128 rows (0 to 127, 128 to 255, ...) at most 24 rows name the same one
- grad_act: bfloat16 [32768, 8, 768], P(('dp', 'expert')), may hold values from -18 to 18
- owner: int32 [64], replicated, may hold values from 0 to 63, as said below
- moves: int32 [2, 2], replicated, may hold values from 0 to 63, as said below
- weight: bfloat16 [64, 2048, 768], P('expert', 'dp'), may hold values from -5 to 5
- first_moment: bfloat16 [64, 2048, 768], P('expert', 'dp'), may hold values from -4 to 4
- second_moment: bfloat16 [64, 2048, 768], P('expert', 'dp'), may hold values from 0.049804688 to 1
- residual: bfloat16 [4, 64, 2048, 768], P('dp', 'expert'), may hold values from -3 to 3
Outputs:
- new_weight: bfloat16 [64, 2048, 768], P('expert', 'dp')
- new_first_moment: bfloat16 [64, 2048, 768], P('expert', 'dp')
- new_second_moment: bfloat16 [64, 2048, 768], P('expert', 'dp')
Inputs may be any that keep to these rules, and one draw needn't show every extreme that they name: `routes`: in each aligned block of 128 rows (the rows of one device) no expert is named by more than 24 rows; in some block some expert is named by exactly 24 rows. `owner`: A permutation: every device of the expert axis owns exactly one expert. `moves`: column 0 lists 2 distinct experts; column 1 gives each its new owner, which is the current owner of another listed expert, so that the listed experts' owners are permuted among themselves and none keeps its own; all other experts keep their owners.
All inputs are finite; a program needn't handle non-finite values.
Results may differ from a plain program's by a relative error of at most 0.018.
Values may be sent and summed in bfloat16 or wider, within the bound.
A program may use at most 128 MiB of HBM per device.

v0:
```python
import jax
import jax.numpy as jnp
from jax import lax
from jax.sharding import PartitionSpec as P

beta_one = 0.9
beta_two = 0.95
step_size = 0.05
epsilon = 1e-08


def silu_slope(values):
    sigma = jax.nn.sigmoid(values)
    return sigma * (1.0 + values * (1.0 - sigma))


def dispatch(tokens, routes, grad_act, holder, peer_count, capacity):
    top_count = routes.shape[1]
    hidden_width = grad_act.shape[2]
    flat_routes = routes.reshape(-1)
    expert_ids = jnp.arange(holder.shape[0], dtype=jnp.int32)
    target = jnp.sum(
        jnp.where(flat_routes[:, None] == expert_ids[None, :], holder[None, :], 0), axis=1
    )
    device_ids = jnp.arange(peer_count, dtype=jnp.int32)
    one_hot = (target[:, None] == device_ids[None, :]).astype(jnp.int32)
    slot_rank = jnp.sum(jnp.cumsum(one_hot, axis=0) * one_hot, axis=1) - 1
    slot_index = target * capacity + slot_rank
    pair_ids = jnp.arange(flat_routes.shape[0], dtype=jnp.int32)
    slot_order = jnp.zeros((peer_count * capacity,), jnp.int32).at[slot_index].set(pair_ids + 1)
    filled = (slot_order > 0)[:, None]
    row_pick = jnp.maximum(slot_order - 1, 0)
    send_rows = jnp.where(filled, tokens[row_pick // top_count], jnp.zeros((), tokens.dtype))
    send_grads = jnp.where(
        filled, grad_act.reshape(-1, hidden_width)[row_pick], jnp.zeros((), grad_act.dtype)
    )
    send_rows = send_rows.reshape(peer_count, capacity, tokens.shape[1])
    send_grads = send_grads.reshape(peer_count, capacity, hidden_width)
    got_rows, got_grads = (
        lax.all_to_all(send_rows, "expert", split_axis=0, concat_axis=0, tiled=True),
        lax.all_to_all(send_grads, "expert", split_axis=0, concat_axis=0, tiled=True),
    )
    return (got_rows.reshape(-1, tokens.shape[1]), got_grads.reshape(-1, hidden_width))


def migrate(owned_state, owner, new_owner, peer_count):
    width_cols = owned_state.shape[1]
    expert_ids = jnp.arange(owner.shape[0], dtype=jnp.int32)
    slot_ids = jnp.arange(peer_count, dtype=jnp.int32)
    held_new = jnp.sum(
        jnp.where(new_owner[None, :] == slot_ids[:, None], expert_ids[None, :], 0), axis=1
    )
    source_slot = jnp.sum(
        jnp.where(held_new[:, None] == expert_ids[None, :], owner[None, :], 0), axis=1
    )
    pieces = owned_state.reshape(1, peer_count, -1, width_cols)
    chosen = lax.all_to_all(pieces, "expert", split_axis=1, concat_axis=0, tiled=True)[source_slot]
    moved_state = lax.all_to_all(chosen, "expert", split_axis=0, concat_axis=1, tiled=True)
    return moved_state.reshape(-1, width_cols)


def update_state(owned_state, rows_x, rows_g, shard_rows, full_rows):
    w_shard = owned_state[:shard_rows]
    m_shard = owned_state[shard_rows : 2 * shard_rows]
    v_shard = owned_state[2 * shard_rows : 3 * shard_rows]
    res_full = owned_state[3 * shard_rows :]
    feature_scale = float(full_rows) ** (-0.5)
    columns = rows_x
    pre_scaled = jnp.dot(
        columns,
        lax.all_gather(w_shard, "dp", axis=0, tiled=True),
        preferred_element_type=jnp.float32,
    )
    pre_act = pre_scaled * feature_scale
    slope_rows = (rows_g.astype(jnp.float32) * silu_slope(pre_act)).astype(jnp.bfloat16)
    columns = rows_x
    partial_grad = (
        lax.dot_general(
            columns, slope_rows, (((0,), (0,)), ((), ())), preferred_element_type=jnp.float32
        )
        * feature_scale
    )
    own_residual = res_full.astype(jnp.float32)
    rounded = (partial_grad + own_residual).astype(jnp.bfloat16)
    grad_total = lax.psum_scatter(
        lax.optimization_barrier(rounded).astype(jnp.float32).astype(jnp.bfloat16),
        "dp",
        scatter_dimension=0,
        tiled=True,
    ).astype(jnp.float32)
    moment_one = beta_one * m_shard.astype(jnp.float32) + (1.0 - beta_one) * grad_total
    moment_two = beta_two * v_shard.astype(jnp.float32) + (1.0 - beta_two) * grad_total * grad_total
    updated = w_shard.astype(jnp.float32) - step_size * moment_one / (
        jnp.sqrt(moment_two) + epsilon
    )
    return (
        updated.astype(jnp.bfloat16),
        moment_one.astype(jnp.bfloat16),
        moment_two.astype(jnp.bfloat16),
    )


def shards(tokens, routes, grad_act, owner, moves, weight, first_moment, second_moment, residual):
    peer_count = lax.axis_size("expert")
    new_owner = owner.at[moves[:, 0]].set(moves[:, 1])
    token_rows, top_count = routes.shape
    capacity = max(2, min(token_rows, 3 * token_rows * top_count // (2 * peer_count)))
    shard_rows = weight.shape[1]
    full_rows = residual.shape[2]
    owned_state = jnp.concatenate(
        [weight[0], first_moment[0], second_moment[0], residual[0, 0]], axis=0
    )
    owned_state = migrate(owned_state, owner, new_owner, peer_count)
    rows_x, rows_g = dispatch(tokens, routes, grad_act, new_owner, peer_count, capacity)
    new_w, new_m, new_v = update_state(owned_state, rows_x, rows_g, shard_rows, full_rows)
    return (new_w[None], new_m[None], new_v[None])


def solution(mesh):
    return jax.shard_map(
        shards,
        mesh=mesh,
        in_specs=(
            P(("dp", "expert"), None),
            P(("dp", "expert"), None),
            P(("dp", "expert"), None, None),
            P(),
            P(),
            P("expert", "dp", None),
            P("expert", "dp", None),
            P("expert", "dp", None),
            P("dp", "expert", None, None),
        ),
        out_specs=(P("expert", "dp", None), P("expert", "dp", None), P("expert", "dp", None)),
        check_vma=False,
    )
```

profile of v0, /device:TPU:36, one launch (start us, length us, event | category | flops | bytes accessed | tf_op | source)
XLA Modules:
  0.0 621.5 jit_solution(12792594530909146742)
XLA Ops:
  7.2 0.0 copy-start
  7.2 6.1 pad_maximum_fusion
  13.3 0.0 copy-start.5
  13.3 0.0 copy-start.6
  13.3 0.0 copy-start.4
  13.3 11.9 %all-to-all-start = ((bf16[1,64,56,768]{3,2,0,1:T(8,128)(2,1)}), bf16[1,64,56,768]{3,2,0,1:T(8,128)(2,1)}, u32[]{:S(2)}, u32[]{:S(2)}) async-start(bf16[1,64,56,768]{3,2,0,1:T(8,128)(2,1)} %bitcast.48), calls=%async_computation | async-start | bytes 11010048 | tf_op jit(solution)/shard_map/all_to_all | solution.py:57
  25.3 0.0 copy-done.5
  25.3 0.1 copy.20
  25.4 0.1 eq.67
  25.5 0.0 copy-done.6
  25.5 0.2 slice_reduce_fusion
  25.6 0.0 copy-done.4
  25.7 0.6 scatter_fusion
  26.2 0.1 select_reduce_fusion
  26.4 18.0 %reduce-window.6 = s32[64,8,128]{2,1,0:T(8,128)S(1)} reduce-window(s32[64,8,128]{2,1,0:T(8,128)S(1)} %fusion.10, s32[]{:T(128)} %constant.17.clone.1), window={size=1x1x128 pad=0_0x0_0x127_0}, to_apply=%region_4.5 | reduce-window | flops 8323072 | bytes 524292 | tf_op jit(solution)/shard_map/reduce-window
  44.4 0.1 slice.40
  44.5 0.1 copy.21
  44.7 0.1 copy.22
  44.8 0.1 broadcast_add_fusion
  44.9 0.1 fusion.9
  45.0 4.3 scatter_custom_fusion.1
  49.4 0.1 broadcast_in_dim.93
  49.5 0.0 copy-done
  49.5 5.7 gather_fusion.2
  55.2 0.0 copy-start.3
  55.2 3.4 broadcast_select_fusion.1
  58.6 88.4 %all-to-all-done = bf16[1,64,56,768]{3,2,0,1:T(8,128)(2,1)} async-done(((bf16[1,64,56,768]{3,2,0,1:T(8,128)(2,1)}), bf16[1,64,56,768]{3,2,0,1:T(8,128)(2,1)}, u32[]{:S(2)}, u32[]{:S(2)}) %all-to-all-start) | async-done | bytes 5505056 | tf_op jit(solution)/shard_map/all_to_all | solution.py:57
  147.0 11.0 %all-to-all-start.3 = ((bf16[64,24,768]{2,1,0:T(8,128)(2,1)}), bf16[64,24,768]{2,1,0:T(8,128)(2,1)}, u32[]{:S(2)}, u32[]{:S(2)}) async-start(bf16[64,24,768]{2,1,0:T(8,128)(2,1)} %broadcast_select_fusion.1), calls=%async_computation.3 | async-start | bytes 4718592 | tf_op jit(solution)/shard_map/all_to_all | solution.py:41
  157.9 0.1 select_reduce_fusion.2
  158.1 0.0 copy-done.3
  158.1 0.2 select_reduce_fusion.1
  158.3 5.9 gather_fusion
  164.1 47.8 %all-to-all-done.3 = bf16[64,24,768]{2,1,0:T(8,128)(2,1)} async-done(((bf16[64,24,768]{2,1,0:T(8,128)(2,1)}), bf16[64,24,768]{2,1,0:T(8,128)(2,1)}, u32[]{:S(2)}, u32[]{:S(2)}) %all-to-all-start.3) | async-done | bytes 2359328 | tf_op jit(solution)/shard_map/all_to_all | solution.py:41
  212.0 0.0 copy-start.2
  212.0 8.7 %all-to-all-start.1 = ((bf16[64,1,56,768]{3,2,1,0:T(8,128)(2,1)}), bf16[64,1,56,768]{3,2,1,0:T(8,128)(2,1)}, u32[]{:S(2)}, u32[]{:S(2)}) async-start(bf16[64,1,56,768]{3,2,1,0:T(8,128)(2,1)} %bitcast.49), calls=%async_computation.1 | async-start | bytes 11010048 | tf_op jit(solution)/shard_map/all_to_all | solution.py:58
  220.7 0.0 copy-done.2
  220.7 7.1 %gather_fusion.1 = bf16[1536,2048]{1,0:T(8,128)(2,1)} fusion(bf16[128,2048]{1,0:T(8,128)(2,1)S(1)} %copy-done.2, s32[2048]{0:T(1024)S(1)} %get-tuple-element.11), kind=kCustom, calls=%fused_computation.1 | custom fusion | bytes 12589056 | tf_op jit(solution)/shard_map/gather | solution.py:33
  227.8 5.9 broadcast_select_fusion
  233.8 107.4 %all-to-all-done.1 = bf16[64,1,56,768]{3,2,1,0:T(8,128)(2,1)} async-done(((bf16[64,1,56,768]{3,2,1,0:T(8,128)(2,1)}), bf16[64,1,56,768]{3,2,1,0:T(8,128)(2,1)}, u32[]{:S(2)}, u32[]{:S(2)}) %all-to-all-start.1) | async-done | bytes 5505056 | tf_op jit(solution)/shard_map/all_to_all | solution.py:58
  341.1 8.8 %all-to-all-start.2 = ((bf16[64,24,2048]{2,1,0:T(8,128)(2,1)}), bf16[64,24,2048]{2,1,0:T(8,128)(2,1)}, u32[]{:S(2)}, u32[]{:S(2)}) async-start(bf16[64,24,2048]{2,1,0:T(8,128)(2,1)} %broadcast_select_fusion), calls=%async_computation.2 | async-start | bytes 12582912 | tf_op jit(solution)/shard_map/all_to_all | solution.py:40
  349.9 0.0 all-gather.2.cloned.1.call-start
  350.0 2.1 slice.38
  352.1 0.0 all-gather.2.cloned.1.call-update
  352.1 0.2 reduce-scatter.2.cloned.1.call-start
  352.3 168.2 %all-to-all-done.2 = bf16[64,24,2048]{2,1,0:T(8,128)(2,1)} async-done(((bf16[64,24,2048]{2,1,0:T(8,128)(2,1)}), bf16[64,24,2048]{2,1,0:T(8,128)(2,1)}, u32[]{:S(2)}, u32[]{:S(2)}) %all-to-all-start.2) | async-done | bytes 6291488 | tf_op jit(solution)/shard_map/all_to_all | solution.py:40
  520.5 0.0 all-gather.2.cloned.1.call-done
  520.5 0.0 copy-start.1
  520.5 21.6 %add_convert_fusion = bf16[2048,768]{1,0:T(8,128)(2,1)} fusion(bf16[1536,2048]{1,0:T(8,128)(2,1)} %bitcast.17, bf16[3584,768]{1,0:T(8,128)(2,1)} %bitcast.10, bf16[1536,768]{1,0:T(8,128)(2,1)} %bitcast.25, bf16[2048,768]{1,0:T(8,128)(2,1)} %all-gather.2.cloned.1.call-done), kind=kOutput, calls=%fused_computation.5 | convolution fusion | flops 9682944000 | bytes 24379392 | tf_op jit(solution)/shard_map/dot_general | solution.py:78
  542.1 0.0 reduce-scatter.2.cloned.1.call-update
  542.1 68.3 %reduce-scatter.2.cloned.1.call-done = bf16[512,768]{1,0:T(8,128)(2,1)} async-done(((bf16[2048,768]{1,0:T(8,128)(2,1)}), bf16[512,768]{1,0:T(8,128)(2,1)}) %reduce-scatter.2.cloned.1.call-update) | async-done | bytes 786448 | tf_op jit(solution)/shard_map/reduce_scatter | solution.py:85
  610.4 4.2 fusion.5
  614.6 0.0 copy-done.1
  (11 shorter events, 0.1 us)
Async XLA Ops:
  7.2 42.3 %copy-start = (bf16[128,8,768]{2,1,0:T(8,128)(2,1)S(1)}, bf16[128,8,768]{2,1,0:T(8,128)(2,1)}, u32[]{:S(2)}) copy-start(bf16[128,8,768]{2,1,0:T(8,128)(2,1)} %param.11) | copy-start | bytes 4718596
  13.3 11.9 %copy-start.5 = (s32[128,8]{0,1:T(8,128)S(1)}, s32[128,8]{0,1:T(8,128)}, u32[]{:S(2)}) copy-start(s32[128,8]{0,1:T(8,128)} %param.10) | copy-start | bytes 12292
  13.3 12.1 %copy-start.6 = (s32[2,2]{1,0:T(2,128)S(1)}, s32[2,2]{1,0:T(2,128)}, u32[]{:S(2)}) copy-start(s32[2,2]{1,0:T(2,128)} %param.13) | copy-start | bytes 52
  13.3 12.3 %copy-start.4 = (s32[64]{0:T(128)S(1)}, s32[64]{0:T(128)}, u32[]{:S(2)}) copy-start(s32[64]{0:T(128)} %param.12) | copy-start | bytes 772
  13.3 133.7 %all-to-all-start = ((bf16[1,64,56,768]{3,2,0,1:T(8,128)(2,1)}), bf16[1,64,56,768]{3,2,0,1:T(8,128)(2,1)}, u32[]{:S(2)}, u32[]{:S(2)}) async-start(bf16[1,64,56,768]{3,2,0,1:T(8,128)(2,1)} %bitcast.48), calls=%async_computation | async-start | bytes 11010048 | tf_op jit(solution)/shard_map/all_to_all | solution.py:57
  55.2 102.9 %copy-start.3 = (s32[64]{0:T(128)S(1)}, s32[64]{0:T(128)}, u32[]{:S(2)}) copy-start(s32[64]{0:T(128)} %param.12) | copy-start | bytes 772
  147.0 65.0 %all-to-all-start.3 = ((bf16[64,24,768]{2,1,0:T(8,128)(2,1)}), bf16[64,24,768]{2,1,0:T(8,128)(2,1)}, u32[]{:S(2)}, u32[]{:S(2)}) async-start(bf16[64,24,768]{2,1,0:T(8,128)(2,1)} %broadcast_select_fusion.1), calls=%async_computation.3 | async-start | bytes 4718592 | tf_op jit(solution)/shard_map/all_to_all | solution.py:41
  212.0 8.8 %copy-start.2 = (bf16[128,2048]{1,0:T(8,128)(2,1)S(1)}, bf16[128,2048]{1,0:T(8,128)(2,1)}, u32[]{:S(2)}) copy-start(bf16[128,2048]{1,0:T(8,128)(2,1)} %param.9) | copy-start | bytes 1572868
  212.0 129.2 %all-to-all-start.1 = ((bf16[64,1,56,768]{3,2,1,0:T(8,128)(2,1)}), bf16[64,1,56,768]{3,2,1,0:T(8,128)(2,1)}, u32[]{:S(2)}, u32[]{:S(2)}) async-start(bf16[64,1,56,768]{3,2,1,0:T(8,128)(2,1)} %bitcast.49), calls=%async_computation.1 | async-start | bytes 11010048 | tf_op jit(solution)/shard_map/all_to_all | solution.py:58
  341.1 179.3 %all-to-all-start.2 = ((bf16[64,24,2048]{2,1,0:T(8,128)(2,1)}), bf16[64,24,2048]{2,1,0:T(8,128)(2,1)}, u32[]{:S(2)}, u32[]{:S(2)}) async-start(bf16[64,24,2048]{2,1,0:T(8,128)(2,1)} %broadcast_select_fusion), calls=%async_computation.2 | async-start | bytes 12582912 | tf_op jit(solution)/shard_map/all_to_all | solution.py:40
  349.9 170.5 %all-gather.2.cloned.1.call-start = ((), (), s32[]{:S(2)}) async-start(), calls=%async_computation.5 | async-start | bytes 3932160 | tf_op jit(solution)/shard_map/all_gather | solution.py:71
  352.1 258.3 %reduce-scatter.2.cloned.1.call-start = ((), (), s32[]{:S(2)}) async-start(), calls=%async_computation.6 | async-start | bytes 3932160 | tf_op jit(solution)/shard_map/reduce_scatter | solution.py:85
  520.5 94.1 %copy-start.1 = (bf16[128,8,768]{2,1,0:T(8,128)(2,1)S(1)}, bf16[128,8,768]{2,1,0:T(8,128)(2,1)}, u32[]{:S(2)}) copy-start(bf16[128,8,768]{2,1,0:T(8,128)(2,1)} %param.11) | copy-start | bytes 4718596
Sparse Core Ops, SparseCore 0:
  353.2 89.9 all-gather.1
  542.2 68.1 reduce-scatter.1
where the time goes:
time: 624 us; the launch traced here: 621 us
  waiting for transfers between devices  480 us (77%)
  starting transfers between devices  40.7 us (7%)
  other arithmetic  38.6 us (6%)
  local copies, waits for them, and re-layouts  26.2 us (4%)
  matrix products  21.6 us (3%)
  between operations  14.3 us (2%)
    all_to_all x1, waiting for transfers between devices, dispatch(): lax.all_to_all(send_rows, 'expert', split_axis=0, concat_axis=0, tiled=True)  168 us
    all_to_all x1, waiting for transfers between devices, migrate(): lax.all_to_all(chosen, 'expert', split_axis=0, concat_axis=1, tiled=True)  107 us
    all_to_all x1, waiting for transfers between devices, migrate(): lax.all_to_all(pieces, 'expert', split_axis=1, concat_axis=0, tiled=True)  88.4 us
    reduce_scatter x1, waiting for transfers between devices, update_state(): lax.psum_scatter(lax.optimization_barrier(rounded).astype(jnp.float32).as...  68.3 us
    all_to_all x1, waiting for transfers between devices, dispatch(): lax.all_to_all(send_grads, 'expert', split_axis=0, concat_axis=0, tiled=T...  47.8 us
    dot_general x1, matrix products, update_state(): lax.dot_general(columns, slope_rows, (((0,), (0,)), ((), ())), preferred_...  21.6 us
    another operation x3, other arithmetic  18.2 us
  transfers between devices with their start and end apart: 6, of which 5 were waited for; matrix products, arithmetic and copies ran while one was open for 9% of the time, Pallas kernels for 0%

commit v1 on v0

v1 whole, which is shorter than its diff:
```python
import functools

import jax
import jax.numpy as jnp
from jax import lax
from jax.experimental import pallas as pl
from jax.experimental.pallas import tpu as pltpu
from jax.sharding import PartitionSpec as P

MESH = pl.DeviceIdType.MESH
F32 = jnp.float32
BF16 = jnp.bfloat16

beta_one = 0.9
beta_two = 0.95
step_size = 0.05
epsilon = 1e-08

NY, NX, NZ = 4, 4, 4
PLANE = NY * NX
CAP = 24
TOP = 8


def silu_slope(values):
    sigma = jax.nn.sigmoid(values)
    return sigma * (1.0 + values * (1.0 - sigma))


def slot_codes(target, ranks, device_col):
    rank = jnp.sum(jnp.where(device_col == target, ranks, 0.0), axis=0, keepdims=True)
    return target * CAP + rank.astype(jnp.int32)


def targets(routes_row, owner_col, device_col):
    return jnp.sum(jnp.where(device_col == routes_row, owner_col, 0), axis=0, keepdims=True)


class Swap:
    def __init__(self, src, places, spot, at, remote, scratch):
        (self.got1, self.kept1, self.got2, self.kept2, self.got3, self.kept3, self.got4, self.back, self.got,
         self.sent, self.come) = scratch
        self.src, self.places, self.at, self.remote = src, places, at, remote
        self.y, self.x, self.z = spot
        self.half = src.shape[1] // 2
        self.piece = self.half // 4
        self.small = self.piece // 4

    def peer(self, half, first, d):
        if first == (half == 0):
            to = lax.rem(self.x + d, NX)
            return to, self.at(self.y * NX + to, self.z), self.x
        to = lax.rem(self.y + d, NY)
        return to, self.at(to * NX + self.x, self.z), self.y

    def where(self, half, first, slot):
        return self.places[2 + 3 * slot + (1 if first == (half == 0) else 0)]

    def rows1(self, half, to):
        return pl.ds(pl.multiple_of(half * self.half + to * self.piece, 16), self.piece)

    def copy1(self, half, d, arriving=False):
        to, device, mine = self.peer(half, True, d)
        return self.remote(self.src.at[:, self.rows1(half, to)], self.got1.at[half, to if arriving else mine],
                           self.sent.at[0, half, to], self.come.at[0, half, to if arriving else mine], device)

    def copy2(self, half, d, arriving=False):
        to, device, mine = self.peer(half, False, d)
        return self.remote(self.kept1.at[half, :, :, pl.ds(pl.multiple_of(to * self.small, 16), self.small)],
                           self.got2.at[half, to if arriving else mine],
                           self.sent.at[1, half, to], self.come.at[1, half, to if arriving else mine], device)

    def copy3(self, half, d, arriving=False):
        to = lax.rem(self.z + d, NZ)
        device = self.at(self.y * NX + self.x, to)
        return self.remote(self.kept2.at[half], self.got3.at[half, to if arriving else self.z],
                           self.sent.at[2, half, to], self.come.at[2, half, to if arriving else self.z], device)

    def copy4(self, half, d, arriving=False):
        to, device, mine = self.peer(half, False, d)
        return self.remote(self.kept3.at[half], self.got4.at[half, to if arriving else mine],
                           self.sent.at[3, half, to], self.come.at[3, half, to if arriving else mine], device)

    def copy5(self, half, d, arriving=False):
        to, device, mine = self.peer(half, True, d)
        return self.remote(self.back.at[half, to], self.got.at[:, self.rows1(half, to if arriving else mine)],
                           self.sent.at[4, half, to], self.come.at[4, half, to if arriving else mine], device)

    def each(self, act):
        for d in (1, 3, 2):
            for half in range(2):
                act(half, d)

    def start(self):
        self.each(lambda half, d: self.copy1(half, d).start())
        for half in range(2):
            mine = self.peer(half, True, 0)[0]
            self.got1[half, mine] = self.src[:, self.rows1(half, mine), :]

    def second(self):
        self.each(lambda half, d: self.copy1(half, d, True).wait_recv())
        for half in range(2):
            for slot in range(2):
                self.kept1[half, slot] = self.got1[half, self.where(half, True, slot)]
        self.each(lambda half, d: self.copy2(half, d).start())
        for half in range(2):
            mine = self.peer(half, False, 0)[0]
            self.got2[half, mine] = self.kept1[half, :, :, pl.ds(pl.multiple_of(mine * self.small, 16), self.small), :]

    def along_z(self):
        self.each(lambda half, d: self.copy2(half, d, True).wait_recv())
        for half in range(2):
            for slot in range(2):
                self.kept2[half, slot] = self.got2[half, self.where(half, False, slot), slot]
        self.each(lambda half, d: self.copy3(half, d).start())
        for half in range(2):
            self.got3[half, self.z] = self.kept2[half]

    def fourth(self):
        self.each(lambda half, d: self.copy3(half, d, True).wait_recv())
        for half in range(2):
            for slot in range(2):
                self.kept3[half, slot] = self.got3[half, self.places[4 + 3 * slot], slot]
        self.each(lambda half, d: self.copy4(half, d).start())
        for half in range(2):
            self.got4[half, self.peer(half, False, 0)[0]] = self.kept3[half]

    def last(self):
        self.each(lambda half, d: self.copy4(half, d, True).wait_recv())
        for d in (1, 3, 2, 0):
            for half in range(2):
                to, device, _ = self.peer(half, True, d)
                slot = jnp.where(self.places[1] == device[1], 0, 1)
                for i in range(4):
                    rows = pl.ds(i * self.small, self.small)
                    if d:
                        self.back[half, to, :, rows, :] = self.got4[half, i, slot]
                    else:
                        first = pl.multiple_of(half * self.half + to * self.piece + i * self.small, 16)
                        self.got[:, pl.ds(first, self.small), :] = self.got4[half, i, slot]
                if d:
                    self.copy5(half, d).start()

    def wait_last(self):
        self.each(lambda half, d: self.copy5(half, d, True).wait_recv())

    def wait_first(self):
        self.each(lambda half, d: self.copy1(half, d).wait_send())

    def wait_sent(self):
        for copy in (self.copy2, self.copy3, self.copy4, self.copy5):
            self.each(lambda half, d: copy(half, d).wait_send())


def swap_scratch(parts, rows, hidden):
    piece, small = rows // 8, rows // 32
    return [
        pltpu.VMEM((2, 4, parts, piece, hidden), BF16),
        pltpu.VMEM((2, 2, parts, piece, hidden), BF16),
        pltpu.VMEM((2, 4, 2, parts, small, hidden), BF16),
        pltpu.VMEM((2, 2, parts, small, hidden), BF16),
        pltpu.VMEM((2, 4, 2, parts, small, hidden), BF16),
        pltpu.VMEM((2, 2, parts, small, hidden), BF16),
        pltpu.VMEM((2, 4, 2, parts, small, hidden), BF16),
        pltpu.VMEM((2, 4, parts, piece, hidden), BF16),
        pltpu.VMEM((parts, rows, hidden), BF16),
        pltpu.SemaphoreType.DMA((5, 2, 4)),
        pltpu.SemaphoreType.DMA((5, 2, 4)),
    ]


def kernel(
    places, routes_t, routes_f, owner_col, tokens, grads, w_shard, m_shard, v_shard, residual,
    w_out, m_out, v_out,
    codes, all_tokens, packed_x, rows_x, packed_g, relay_g, rows_g, w_full, pre, slopes,
    term, pair_got, z_send, z_got,
    local_sem, tok_up, tok_dn, tok_got, code_up, code_dn, code_got,
    x_sent, x_got, g_sent, g_got, gz_sent, gz_got, w_sent, w_got, t_sent, t_got,
    added, state, grad_small, *swaps,
):
    count = owner_col.shape[0]
    tok_rows, feats = tokens.shape
    hidden = grads.shape[1]
    pairs = grads.shape[0]
    shard_rows = w_shard.shape[0]
    scale = float(feats) ** -0.5

    dp = lax.axis_index("dp")
    me = lax.axis_index("expert")
    z_hi, core = dp // 2, dp % 2
    yx, z = me // NZ, me % NZ
    y, x = yx // NX, yx % NX

    def at(yx_to, z_to):
        return (dp, yx_to * NZ + z_to)

    core_peer = (z_hi * 2 + 1 - core, me)
    far_peer = ((1 - z_hi) * 2 + core, me)

    def plane_peer(dy, dx):
        return lax.rem(y + dy, NY) * NX + lax.rem(x + dx, NX)

    def remote(src, dst, sent, got, to):
        return pltpu.make_async_remote_copy(
            src_ref=src, dst_ref=dst, send_sem=sent, recv_sem=got, device_id=to, device_id_type=MESH
        )

    offsets = [(dy, dx) for dy in range(NY) for dx in range(NX) if dy or dx]

    loads = [
        pltpu.make_async_copy(tokens, all_tokens.at[z], local_sem.at[4]),
        pltpu.make_async_copy(w_shard, state.at[0], local_sem.at[5]),
        pltpu.make_async_copy(m_shard, state.at[1], local_sem.at[6]),
        pltpu.make_async_copy(v_shard, state.at[2], local_sem.at[7]),
        pltpu.make_async_copy(residual, added, local_sem.at[8]),
    ]
    for load in loads:
        load.start()

    barrier = pltpu.get_barrier_semaphore()
    for dy, dx in offsets:
        pl.semaphore_signal(barrier, inc=1, device_id=at(plane_peer(dy, dx), z), device_id_type=MESH)
    for dz in range(1, NZ):
        pl.semaphore_signal(barrier, inc=1, device_id=at(yx, lax.rem(z + dz, NZ)), device_id_type=MESH)
    pl.semaphore_signal(barrier, inc=1, device_id=core_peer, device_id_type=MESH)
    pl.semaphore_signal(barrier, inc=1, device_id=far_peer, device_id_type=MESH)
    pl.semaphore_wait(barrier, len(offsets) + NZ - 1 + 2)

    device_col = lax.broadcasted_iota(jnp.int32, (count, 1), 0)
    own_col = owner_col[...]
    before = (
        lax.broadcasted_iota(jnp.int32, (tok_rows, tok_rows), 0)
        < lax.broadcasted_iota(jnp.int32, (tok_rows, tok_rows), 1)
    ).astype(F32).astype(BF16)
    row_targets = [targets(routes_t[k : k + 1, :], own_col, device_col) for k in range(TOP)]
    member = jnp.zeros((count, tok_rows), F32)
    for k in range(TOP):
        member = member + jnp.where(device_col == row_targets[k], 1.0, 0.0)
    ranks = jnp.dot(member.astype(BF16), before, preferred_element_type=F32)
    codes[z] = jnp.concatenate([slot_codes(t, ranks, device_col) for t in row_targets], axis=0)
    loads[0].wait()

    def hop(source, up):
        step = 1 if up else -1
        to = at(yx, z + step)
        sems = (tok_up, code_up) if up else (tok_dn, code_dn)
        return (
            remote(all_tokens.at[source], all_tokens.at[source], sems[0].at[source], tok_got.at[source], to),
            remote(codes.at[source], codes.at[source], sems[1].at[source], code_got.at[source], to),
        )

    def send_hop(source):
        @pl.when((source <= z) & (z < NZ - 1))
        def _():
            for copy in hop(source, True):
                copy.start()

        @pl.when((source >= z) & (z > 0))
        def _():
            for copy in hop(source, False):
                copy.start()

    def wait_hop(source, up):
        for copy in hop(source, up):
            copy.wait_recv()

    send_hop(z)

    ranked = []
    carry = jnp.zeros((count, 1), F32)
    flat_target = targets(routes_f[...], own_col, device_col)
    for c in range(pairs // tok_rows):
        part = flat_target[:, c * tok_rows : (c + 1) * tok_rows]
        hits = jnp.where(device_col == part, 1.0, 0.0)
        ranked.append(jnp.dot(hits.astype(BF16), before, preferred_element_type=F32) + carry)
        carry = carry + jnp.sum(hits, axis=1, keepdims=True)
    flat_codes = slot_codes(flat_target, jnp.concatenate(ranked, axis=1), device_col)

    group = NX * NZ * CAP

    def g_plane(to):
        return remote(packed_g.at[to], relay_g.at[yx], g_sent.at[to], g_got.at[yx], at(to, z))

    for dy in range(NY):
        y_to = lax.rem(y + dy, NY)
        slot = lax.broadcasted_iota(jnp.int32, (group, pairs), 0) + y_to * group
        pick = jnp.where(slot == flat_codes, 1.0, 0.0).astype(BF16)
        got = jnp.dot(pick, grads[...], preferred_element_type=F32)
        for x_to in range(NX):
            for z_to in range(NZ):
                first = (x_to * NZ + z_to) * CAP
                packed_g[y_to * NX + x_to, z_to] = got[first : first + CAP].astype(BF16)
        for dx in range(NX):
            if dy or dx:
                g_plane(plane_peer(dy, dx)).start()
    self_g = pltpu.make_async_copy(packed_g.at[yx], relay_g.at[yx], local_sem.at[0])
    self_g.start()

    block = 2 * CAP

    def x_plane(pair, to):
        return remote(
            packed_x.at[pair, pl.ds(to * block, block)],
            rows_x.at[pl.ds((pair * PLANE + yx) * block, block)],
            x_sent.at[pair, to], x_got.at[pair, yx], at(to, z),
        )

    def pack_pair(pair, slot):
        part = NX * block
        s = lax.broadcasted_iota(jnp.int32, (part, tok_rows), 0)
        to = (s * 1366) >> 16
        half = (s * 2731) >> 16
        for dy in range(NY):
            y_to = lax.rem(y + dy, NY)
            rank = s - half * CAP
            want = ((y_to * NX + to) * NZ + z) * CAP + rank
            picks = []
            for sub in range(2):
                source = codes[pair * 2 + sub]
                mine = jnp.where(half == 2 * to + sub, want, -1)
                hit = jnp.zeros((part, tok_rows), F32)
                for k in range(TOP):
                    hit = hit + jnp.where(mine == source[k : k + 1, :], 1.0, 0.0)
                picks.append(hit.astype(BF16))
            pick = jnp.concatenate(picks, axis=1)
            both = all_tokens[pl.ds(pair * 2, 2)].reshape(2 * tok_rows, feats)
            rows = pl.ds(pl.multiple_of(y_to * part, 16), part)
            packed_x[pair, rows, :] = jnp.dot(pick, both, preferred_element_type=F32).astype(BF16)
            for dx in range(NX):
                if dy or dx:
                    x_plane(pair, plane_peer(dy, dx)).start()
        pltpu.make_async_copy(
            packed_x.at[pair, pl.ds(yx * block, block)],
            rows_x.at[pl.ds((pair * PLANE + yx) * block, block)],
            local_sem.at[slot],
        ).start()

    def wait_pair(pair, slot):
        for dy, dx in offsets:
            src = plane_peer(dy, dx)
            remote(
                packed_x.at[pair, pl.ds(src * block, block)],
                rows_x.at[pl.ds((pair * PLANE + src) * block, block)],
                x_sent.at[pair, src], x_got.at[pair, src], at(src, z),
            ).wait_recv()
        pltpu.make_async_copy(
            packed_x.at[pair, pl.ds(yx * block, block)],
            rows_x.at[pl.ds((pair * PLANE + yx) * block, block)],
            local_sem.at[slot],
        ).wait()

    def take_hop(distance):
        @pl.when(z >= distance)
        def _():
            wait_hop(z - distance, True)
            send_hop(z - distance)

        @pl.when(z + distance < NZ)
        def _():
            wait_hop(z + distance, False)
            send_hop(z + distance)

    my_pair = z // 2
    take_hop(1)
    pack_pair(my_pair, 1)
    take_hop(2)

    def w_rows(owner_dp):
        return w_full.at[pl.ds(pl.multiple_of(owner_dp * shard_rows, 16), shard_rows)]

    for load in loads[1:4]:
        load.wait()
    w_full[pl.ds(pl.multiple_of(dp * shard_rows, 16), shard_rows), :] = state[0]
    far_dp = (1 - z_hi) * 2 + core
    near_dp = z_hi * 2 + 1 - core
    w_far = remote(state.at[0], w_rows(dp), w_sent.at[0], w_got.at[0], far_peer)
    w_near = remote(state.at[0], w_rows(dp), w_sent.at[1], w_got.at[1], core_peer)
    w_pass = remote(w_rows(far_dp), w_rows(far_dp), w_sent.at[2], w_got.at[2], core_peer)
    w_far.start()
    w_near.start()

    take_hop(3)
    pack_pair(1 - my_pair, 2)

    half_swap = len(swaps) // 2
    swap_state = Swap(state, places, (y, x, z), at, remote, swaps[:half_swap])
    swap_grad = Swap(grad_small, places, (y, x, z), at, remote, swaps[half_swap:])
    swap_state.start()

    for dy, dx in offsets:
        src = plane_peer(dy, dx)
        remote(packed_g.at[src], relay_g.at[src], g_sent.at[src], g_got.at[src], at(src, z)).wait_recv()
    self_g.wait()

    def g_line(z_to, z_from):
        return remote(relay_g.at[:, z_to], rows_g.at[z_from], gz_sent.at[z_to], gz_got.at[z_from], at(yx, z_to))

    for dz in range(1, NZ):
        g_line(lax.rem(z + dz, NZ), z).start()
    self_rows = pltpu.make_async_copy(relay_g.at[:, z], rows_g.at[z], local_sem.at[3])
    self_rows.start()

    w_far.wait_recv()
    w_pass.start()
    w_near.wait_recv()
    w_pass.wait_recv()

    def wait_line(z_from):
        remote(
            relay_g.at[:, z_from], rows_g.at[z_from], gz_sent.at[z_from], gz_got.at[z_from], at(yx, z_from)
        ).wait_recv()

    def forward(pair):
        per = PLANE // 2
        for part in range(2):
            base = pl.multiple_of((pair * PLANE + part * per) * block, 16)
            pre[pl.ds(0, per * block), :] = jnp.dot(
                rows_x[pl.ds(base, per * block), :], w_full[...], preferred_element_type=F32
            ) * scale

            def body(i, _):
                rows = pl.ds(pl.multiple_of(i * block, 16), block)
                src = part * per + i
                g = jnp.concatenate(
                    [rows_g[pair * 2, src].astype(F32), rows_g[pair * 2 + 1, src].astype(F32)], axis=0
                )
                slope = (g * silu_slope(pre[rows, :])).astype(BF16)
                slopes[pl.ds(pl.multiple_of(base + i * block, 16), block), :] = slope
                return 0

            lax.fori_loop(0, per, body, 0)

    wait_pair(my_pair, 1)
    for dz in range(1, NZ):
        wait_line(lax.rem(z + dz, NZ))
    self_rows.wait()
    forward(my_pair)
    wait_pair(1 - my_pair, 2)
    forward(1 - my_pair)
    swap_state.second()

    tile = shard_rows // 2

    def gradient(shard):
        def body(i, _):
            first = pl.multiple_of(shard * shard_rows + i * tile, 128)
            part = lax.dot_general(
                rows_x[:, pl.ds(first, tile)], slopes[...], (((0,), (0,)), ((), ())),
                preferred_element_type=F32,
            )
            total = part * scale + added[pl.ds(first, tile), :].astype(F32)
            term[shard, pl.ds(pl.multiple_of(i * tile, 16), tile), :] = total.astype(BF16)
            return 0

        lax.fori_loop(0, 2, body, 0)

    def to_core(z_hi_of):
        shard = z_hi_of * 2 + 1 - core
        return remote(term.at[shard], pair_got.at[z_hi_of], t_sent.at[z_hi_of], t_got.at[z_hi_of], core_peer)

    loads[4].wait()
    gradient(far_dp + 1 - 2 * core)
    to_core(1 - z_hi).start()
    gradient(far_dp)
    to_core(1 - z_hi).wait_recv()
    z_send[...] = (term[far_dp].astype(F32) + pair_got[1 - z_hi].astype(F32)).astype(BF16)
    z_copy = remote(z_send, z_got, t_sent.at[2], t_got.at[2], far_peer)
    z_copy.start()
    swap_state.along_z()
    gradient(near_dp)
    to_core(z_hi).start()
    gradient(dp)
    swap_state.fourth()
    to_core(z_hi).wait_recv()
    z_copy.wait_recv()
    grad_total = pre
    grad_total[pl.ds(0, shard_rows), :] = term[dp].astype(F32) + pair_got[z_hi].astype(F32) + z_got[...].astype(F32)
    grad_small[0] = grad_total[pl.ds(0, shard_rows), :].astype(BF16)

    swap_grad.start()
    swap_state.last()
    swap_grad.second()
    swap_grad.along_z()
    swap_grad.fourth()
    swap_grad.last()
    swap_state.wait_last()
    swap_grad.wait_last()

    swap_state.wait_first()
    w_far.wait_send()
    w_near.wait_send()
    moved = (places[0] == me) | (places[1] == me)

    def update(i, _):
        rows = pl.ds(pl.multiple_of(i * 64, 16), 64)
        total = jnp.where(moved, swap_grad.got[0, rows, :].astype(F32), grad_total[rows, :])
        old = [
            jnp.where(moved, swap_state.got[c, rows, :].astype(F32), state[c, rows, :].astype(F32))
            for c in range(3)
        ]
        moment_one = beta_one * old[1] + (1.0 - beta_one) * total
        moment_two = beta_two * old[2] + (1.0 - beta_two) * total * total
        state[0, rows, :] = (old[0] - step_size * moment_one / (jnp.sqrt(moment_two) + epsilon)).astype(BF16)
        state[1, rows, :] = moment_one.astype(BF16)
        state[2, rows, :] = moment_two.astype(BF16)
        return 0

    lax.fori_loop(0, shard_rows // 64, update, 0)
    stores = [
        pltpu.make_async_copy(state.at[c], out, local_sem.at[5 + c]) for c, out in enumerate((w_out, m_out, v_out))
    ]
    for store in stores:
        store.start()

    for source in range(NZ):

        @pl.when((source <= z) & (z < NZ - 1))
        def _():
            for copy in hop(source, True):
                copy.wait_send()

        @pl.when((source >= z) & (z > 0))
        def _():
            for copy in hop(source, False):
                copy.wait_send()

    for dy, dx in offsets:
        to = plane_peer(dy, dx)
        g_plane(to).wait_send()
        for pair in range(2):
            x_plane(pair, to).wait_send()
    for dz in range(1, NZ):
        g_line(lax.rem(z + dz, NZ), z).wait_send()
    w_pass.wait_send()
    to_core(0).wait_send()
    to_core(1).wait_send()
    z_copy.wait_send()
    swap_state.wait_sent()
    swap_grad.wait_first()
    swap_grad.wait_sent()
    for store in stores:
        store.wait()


def expert_update(tokens, routes, grads, owner, moves, w_shard, m_shard, v_shard, residual):
    tok_rows, feats = tokens.shape
    hidden = grads.shape[1]
    count = owner.shape[0]
    shard_rows = w_shard.shape[0]
    rows = count * CAP
    dma = pltpu.SemaphoreType.DMA
    vmem = pl.BlockSpec(memory_space=pltpu.VMEM)
    hbm = pl.BlockSpec(memory_space=pl.ANY)
    pair = jnp.stack([moves[1, 1], moves[0, 1]])
    spots = jnp.stack([pair // (NX * NZ), (pair // NZ) % NX, pair % NZ], axis=1)
    places = jnp.concatenate([pair, spots.reshape(-1)])
    return pl.pallas_call(
        kernel,
        out_shape=[jax.ShapeDtypeStruct((shard_rows, hidden), BF16)] * 3,
        in_specs=[
            pl.BlockSpec(memory_space=pltpu.SMEM), vmem, vmem, vmem, hbm, vmem, hbm, hbm, hbm, hbm
        ],
        out_specs=[hbm] * 3,
        scratch_shapes=[
            pltpu.VMEM((NZ, TOP, tok_rows), jnp.int32),
            pltpu.VMEM((NZ, tok_rows, feats), BF16),
            pltpu.VMEM((2, rows // 2, feats), BF16),
            pltpu.VMEM((rows, feats), BF16),
            pltpu.VMEM((PLANE, NZ, CAP, hidden), BF16),
            pltpu.VMEM((PLANE, NZ, CAP, hidden), BF16),
            pltpu.VMEM((NZ, PLANE, CAP, hidden), BF16),
            pltpu.VMEM((feats, hidden), BF16),
            pltpu.VMEM((max(rows // 4, shard_rows), hidden), F32),
            pltpu.VMEM((rows, hidden), BF16),
            pltpu.VMEM((4, shard_rows, hidden), BF16),
            pltpu.VMEM((2, shard_rows, hidden), BF16),
            pltpu.VMEM((shard_rows, hidden), BF16),
            pltpu.VMEM((shard_rows, hidden), BF16),
            dma((9,)),
            dma((NZ,)), dma((NZ,)), dma((NZ,)), dma((NZ,)), dma((NZ,)), dma((NZ,)),
            dma((2, PLANE)), dma((2, PLANE)), dma((PLANE,)), dma((PLANE,)), dma((NZ,)), dma((NZ,)),
            dma((3,)), dma((3,)), dma((3,)), dma((3,)),
            pltpu.VMEM((feats, hidden), BF16),
            pltpu.VMEM((3, shard_rows, hidden), BF16),
            pltpu.VMEM((1, shard_rows, hidden), BF16),
            *swap_scratch(3, shard_rows, hidden),
            *swap_scratch(1, shard_rows, hidden),
        ],
        compiler_params=pltpu.CompilerParams(
            collective_id=0, has_side_effects=True, vmem_limit_bytes=62 * 2**20
        ),
        name="expert_update",
    )(
        places, routes.T, routes.reshape(1, -1), owner[:, None], tokens, grads, w_shard, m_shard, v_shard, residual
    )


def shards(tokens, routes, grad_act, owner, moves, weight, first_moment, second_moment, residual):
    hidden = grad_act.shape[2]
    new_w, new_m, new_v = expert_update(
        tokens, routes, grad_act.reshape(-1, hidden), owner, moves, weight[0], first_moment[0], second_moment[0],
        residual[0, 0],
    )
    return (new_w[None], new_m[None], new_v[None])


def solution(mesh):
    return jax.shard_map(
        shards,
        mesh=mesh,
        in_specs=(
            P(("dp", "expert"), None),
            P(("dp", "expert"), None),
            P(("dp", "expert"), None, None),
            P(),
            P(),
            P("expert", "dp", None),
            P("expert", "dp", None),
            P("expert", "dp", None),
            P("dp", "expert", None, None),
        ),
        out_specs=(P("expert", "dp", None), P("expert", "dp", None), P("expert", "dp", None)),
        check_vma=False,
    )
```

time: 624 us -> 278 us (0.45)
  waiting for transfers between devices: 480 us -> 0 us
  Pallas kernels: 0 us -> 263 us
  starting transfers between devices: 40.7 us -> 0 us
  other arithmetic: 38.6 us -> 4.58 us
  matrix products: 21.6 us -> 0 us
  local copies, waits for them, and re-layouts: 26.2 us -> 9.34 us
  between operations: 14.3 us -> 0.66 us
    all_to_all x4 -> x0, waiting for transfers between devices: 412 us -> none  [the longest x1 168 us: dispatch(): lax.all_to_all(send_rows, 'expert', split_axis=0, concat_axis=0, tiled=True)]
    pallas_call x0 -> x1, Pallas kernels: none -> 263 us  [expert_update(): pl.pallas_call(kernel, out_shape=[jax.ShapeDtypeStruct((shard_rows, hidde...]
    reduce_scatter x1 -> x0, waiting for transfers between devices: 68.3 us -> none  [update_state(): lax.psum_scatter(lax.optimization_barrier(rounded).astype(jnp.float32).as...]
    all_to_all x4 -> x0, starting transfers between devices: 40.4 us -> none  [the longest x1 11.9 us: migrate(): lax.all_to_all(pieces, 'expert', split_axis=1, concat_axis=0, tiled=True)]
    dot_general x1 -> x0, matrix products: 21.6 us -> none  [update_state(): lax.dot_general(columns, slope_rows, (((0,), (0,)), ((), ())), preferred_...]
    gather x3 -> x0, local copies, waits for them, and re-layouts: 18.6 us -> none  [the longest x1 7.09 us: dispatch(): tokens[row_pick // top_count]]
    another operation x3 -> x1, other arithmetic: 18.2 us -> 0.08 us  [expert_update(): spots = jnp.stack([pair // (NX * NZ), pair // NZ % NX, pair % NZ], axis=1)]
    select_n x4 -> x2, other arithmetic: 9.39 us -> 2.62 us  [expert_update(): spots = jnp.stack([pair // (NX * NZ), pair // NZ % NX, pair % NZ], axis=1)]
  transfers between devices with their start and end apart: 6 -> 0, of which waited for: 5 -> 0; matrix products, arithmetic and copies ran while one was open for 9% -> 0% of each run, Pallas kernels for 0% -> 0%
where the time goes in v1:
time: 278 us
  Pallas kernels  263 us (95%)
  local copies, waits for them, and re-layouts  9.34 us (3%)
  other arithmetic  4.58 us (2%)
    pallas_call x1, Pallas kernels, expert_update(): pl.pallas_call(kernel, out_shape=[jax.ShapeDtypeStruct((shard_rows, hidde...  263 us
    unnamed x6, local copies, waits for them, and re-layouts  5.87 us

profile of v1, /device:TPU:36, one launch (start us, length us, event | category | flops | bytes accessed | tf_op | source)
XLA Modules:
  0.0 277.5 jit_solution(11681600737827736275)
XLA Ops:
  0.6 1.3 fusion.1
  2.0 1.3 and_select_fusion.3
  3.3 1.3 and_select_fusion
  4.6 0.1 pad_add_fusion.1
  4.7 0.1 reshape.316
  4.8 1.9 pad_add_fusion.2.places
  6.6 1.4 copy.15.owner_col
  8.0 0.8 copy.14
  8.8 0.7 reshape.317.routes_f
  9.5 262.9 %expert_update.1 = (bf16[512,768]{1,0:T(8,128)(2,1)}, bf16[512,768]{1,0:T(8,128)(2,1)}, bf16[512,768]{1,0:T(8,128)(2,1)}) custom-call(s32[8]{0:T(128)} %pad_add_fusion.2.places, s32[8,128]{1,0:T(8,128)} %bitcast.20, s32[1,1024]{1,0:T(1,128)} %reshape.317.routes_f, s32[64,1]{1,0:T(8,128)} %copy.15.owner_col, bf16[128,2048]{1,0:T(8,128)(2,1)} %tokens.1, ...), custom_call_target="tpu_custom_call" | custom-call | tf_op jit(solution)/shard_map/expert_update/pallas_call | solution.py:557
  272.4 0.0 copy-start
  272.4 2.1 copy.19
  274.6 2.1 copy.20
  276.6 0.0 copy-done
  276.6 0.9 copy.21
Async XLA Ops:
  272.4 4.2 %copy-start = (bf16[512,768]{1,0:T(8,128)(2,1)S(1)}, bf16[512,768]{1,0:T(8,128)(2,1)}, u32[]{:S(2)}) copy-start(bf16[512,768]{1,0:T(8,128)(2,1)} %get-tuple-element.8) | copy-start | bytes 2359300

commit v2 on v1

v2 whole, which is shorter than its diff:
```python
import functools

import jax
import jax.numpy as jnp
from jax import lax
from jax.experimental import pallas as pl
from jax.experimental.pallas import tpu as pltpu
from jax.sharding import PartitionSpec as P

MESH = pl.DeviceIdType.MESH
F32 = jnp.float32
BF16 = jnp.bfloat16

beta_one = 0.9
beta_two = 0.95
step_size = 0.05
epsilon = 1e-08

NY, NX, NZ = 4, 4, 4
PLANE = NY * NX
CAP = 24
TOP = 8


def silu_slope(values):
    sigma = jax.nn.sigmoid(values)
    return sigma * (1.0 + values * (1.0 - sigma))


class Swap:
    def __init__(self, src, pair, spot, at, remote, scratch):
        (self.got1, self.out2, self.got2, self.out3, self.got3, self.out4, self.got4, self.back, self.got,
         self.sent, self.come) = scratch
        self.src, self.pair, self.at, self.remote = src, pair, at, remote
        self.y, self.x, self.z = spot
        self.ys = [p // (NX * NZ) for p in pair]
        self.xs = [(p // NZ) % NX for p in pair]
        self.zs = [p % NZ for p in pair]
        self.half = src.shape[1] // 2
        self.piece = self.half // 4
        self.small = self.piece // 4

    def axes(self, half):
        along = [(self.x, self.xs), (self.y, self.ys)]
        return along if half == 0 else along[::-1]

    def peer(self, half, first, d):
        if first == (half == 0):
            to = lax.rem(self.x + d, NX)
            return to, self.at(self.y * NX + to, self.z), self.x
        to = lax.rem(self.y + d, NY)
        return to, self.at(to * NX + self.x, self.z), self.y

    def rows1(self, half, to):
        return pl.ds(pl.multiple_of(half * self.half + to * self.piece, 16), self.piece)

    def rows2(self, to):
        return pl.ds(pl.multiple_of(to * self.small, 16), self.small)

    def copy1(self, half, d, arriving=False):
        to, device, mine = self.peer(half, True, d)
        return self.remote(self.src.at[:, self.rows1(half, to)], self.got1.at[half, to if arriving else mine],
                           self.sent.at[0, half, to], self.come.at[0, half, to if arriving else mine], device)

    def copy2(self, half, d, arriving=False):
        to, device, mine = self.peer(half, False, d)
        return self.remote(self.out2.at[half, :, self.rows2(to)], self.got2.at[half, to if arriving else mine],
                           self.sent.at[1, half, to], self.come.at[1, half, to if arriving else mine], device)

    def copy3(self, half, d, arriving=False):
        to = lax.rem(self.z + d, NZ)
        device = self.at(self.y * NX + self.x, to)
        mine = to if arriving else self.z
        return self.remote(self.out3.at[half], self.got3.at[half, mine],
                           self.sent.at[2, half, to], self.come.at[2, half, mine], device)

    def copy4(self, half, d, arriving=False):
        to, device, mine = self.peer(half, False, d)
        return self.remote(self.out4.at[half, to], self.got4.at[half, to if arriving else mine],
                           self.sent.at[3, half, to], self.come.at[3, half, to if arriving else mine], device)

    def copy5(self, half, d, arriving=False):
        to, device, mine = self.peer(half, True, d)
        return self.remote(self.back.at[half, to], self.got.at[:, self.rows1(half, to if arriving else mine)],
                           self.sent.at[4, half, to], self.come.at[4, half, to if arriving else mine], device)

    def each(self, act):
        for d in (1, 3, 2):
            for half in range(2):
                act(half, d)

    def start(self):
        self.each(lambda half, d: self.copy1(half, d).start())
        for half in range(2):
            mine = self.peer(half, True, 0)[0]
            self.got1[half, mine] = self.src[:, self.rows1(half, mine), :]

    def second(self):
        self.each(lambda half, d: self.copy1(half, d, True).wait_recv())
        for half in range(2):
            (_, firsts), (second, seconds) = self.axes(half)
            held = (second == seconds[0]) & (self.z == self.zs[0])
            self.out2[half] = self.got1[half, jnp.where(held, firsts[0], firsts[1])]
        self.each(lambda half, d: self.copy2(half, d).start())
        for half in range(2):
            mine = self.peer(half, False, 0)[0]
            self.got2[half, mine] = self.out2[half, :, self.rows2(mine), :]

    def along_z(self):
        self.each(lambda half, d: self.copy2(half, d, True).wait_recv())
        for half in range(2):
            seconds = self.axes(half)[1][1]
            self.out3[half] = self.got2[half, jnp.where(self.z == self.zs[0], seconds[0], seconds[1])]
        self.each(lambda half, d: self.copy3(half, d).start())
        for half in range(2):
            self.got3[half, self.z] = self.out3[half]

    def fourth(self):
        self.each(lambda half, d: self.copy3(half, d, True).wait_recv())
        plane = self.zs[0] == self.zs[1]
        for d in (1, 3, 2, 0):
            for half in range(2):
                seconds = self.axes(half)[1][1]
                to = self.peer(half, False, d)[0]
                takes = (to == seconds[1]) & (self.z == self.zs[1])
                kept = jnp.where(
                    plane,
                    self.got2[half, jnp.where(takes, seconds[0], seconds[1])],
                    self.got3[half, jnp.where(takes, self.zs[0], self.zs[1])],
                )
                if d:
                    self.out4[half, to] = kept
                    self.copy4(half, d).start()
                else:
                    self.got4[half, to] = kept

    def last(self):
        self.each(lambda half, d: self.copy4(half, d, True).wait_recv())
        for d in (1, 3, 2, 0):
            for half in range(2):
                (_, firsts), (_, seconds) = self.axes(half)
                row = (seconds[0] == seconds[1]) & (self.zs[0] == self.zs[1])
                to, device, _ = self.peer(half, True, d)
                index = jnp.where(self.pair[1] == device[1], firsts[0], firsts[1])
                for i in range(4):
                    rows = pl.ds(i * self.small, self.small)
                    part = jnp.where(row, self.got1[half, index, :, rows, :], self.got4[half, i])
                    if d:
                        self.back[half, to, :, rows, :] = part
                    else:
                        first = pl.multiple_of(half * self.half + to * self.piece + i * self.small, 16)
                        self.got[:, pl.ds(first, self.small), :] = part
                if d:
                    self.copy5(half, d).start()

    def wait_last(self):
        self.each(lambda half, d: self.copy5(half, d, True).wait_recv())

    def wait_first(self):
        self.each(lambda half, d: self.copy1(half, d).wait_send())

    def wait_sent(self):
        for copy in (self.copy2, self.copy3, self.copy4, self.copy5):
            self.each(lambda half, d: copy(half, d).wait_send())


class Route:
    def __init__(self, spot, at, remote, send, relay, own, passed, dest, sems):
        self.y, self.x, self.z = spot
        self.at, self.remote = at, remote
        self.send, self.relay, self.own, self.passed, self.dest = send, relay, own, passed, dest
        self.sent1, self.got1, self.sent2, self.got2, self.local = sems

    def spots(self, half):
        return (self.x, self.y) if half == 0 else (self.y, self.x)

    def device(self, half, first, to):
        along_x = first == (half == 0)
        return self.at(self.y * NX + to if along_x else to * NX + self.x, self.z)

    def hop1(self, half, d, arriving=False):
        mine = self.spots(half)[0]
        to = lax.rem(mine + d, 4)
        index = to if arriving else mine
        return self.remote(self.send(half, to), self.relay(half, index), self.sent1.at[half, to],
                           self.got1.at[half, index], self.device(half, True, to))

    def hop2(self, half, d, e, arriving=False):
        first, second = self.spots(half)
        come = lax.rem(first + d, 4)
        to = lax.rem(second + e, 4)
        piece = self.passed(half, come, to) if d else self.own(half, to)
        if not e:
            return pltpu.make_async_copy(piece, self.dest(half, come, second), self.local.at[half, come])
        index = to if arriving else second
        return self.remote(piece, self.dest(half, come, index), self.sent2.at[half, come, to],
                           self.got2.at[half, come, index], self.device(half, False, to))

    def start(self):
        for d in (1, 3, 2):
            for half in range(2):
                self.hop1(half, d).start()
        self.pass_on(0)

    def pass_on(self, d):
        for half in range(2):
            if d:
                self.hop1(half, d, True).wait_recv()
            for e in (1, 3, 2, 0):
                self.hop2(half, d, e).start()

    def relay_all(self):
        for d in (1, 3, 2):
            self.pass_on(d)

    def wait_all(self):
        for half in range(2):
            for d in range(4):
                for e in range(1, 4):
                    self.hop2(half, d, e, True).wait_recv()
                self.hop2(half, d, 0).wait()

    def wait_sent(self):
        for half in range(2):
            for d in range(4):
                if d:
                    self.hop1(half, d).wait_send()
                for e in range(1, 4):
                    self.hop2(half, d, e).wait_send()


def route_sems():
    dma = pltpu.SemaphoreType.DMA
    return [dma((2, 4)), dma((2, 4)), dma((2, 4, 4)), dma((2, 4, 4)), dma((2, 4))]


def swap_scratch(parts, rows, hidden):
    piece, small = rows // 8, rows // 32
    return [
        pltpu.VMEM((2, 4, parts, piece, hidden), BF16),
        pltpu.VMEM((2, parts, piece, hidden), BF16),
        pltpu.VMEM((2, 4, parts, small, hidden), BF16),
        pltpu.VMEM((2, parts, small, hidden), BF16),
        pltpu.VMEM((2, 4, parts, small, hidden), BF16),
        pltpu.VMEM((2, 4, parts, small, hidden), BF16),
        pltpu.VMEM((2, 4, parts, small, hidden), BF16),
        pltpu.VMEM((2, 4, parts, piece, hidden), BF16),
        pltpu.VMEM((parts, rows, hidden), BF16),
        pltpu.SemaphoreType.DMA((5, 2, 4)),
        pltpu.SemaphoreType.DMA((5, 2, 4)),
    ]


def kernel(
    moves, routes_t, owner_row, tokens, grads, w_shard, m_shard, v_shard, residual,
    w_out, m_out, v_out,
    codes, all_tokens, packed_x, relay_x, rows_x, packed_g, passed_g, relay_g, rows_g, w_full, pre, slopes,
    term, pair_got, z_send, z_got,
    local_sem, tok_up, tok_dn, tok_got, code_up, code_dn, code_got,
    gz_sent, gz_got, w_sent, w_got, t_sent, t_got,
    state, grad_small, *rest,
):
    count = owner_row.shape[1]
    tok_rows, feats = tokens.shape
    hidden = grads.shape[1]
    pairs = grads.shape[0]
    shard_rows = w_shard.shape[0]
    scale = float(feats) ** -0.5

    dp = lax.axis_index("dp")
    me = lax.axis_index("expert")
    z_hi, core = dp // 2, dp % 2
    yx, z = me // NZ, me % NZ
    y, x = yx // NX, yx % NX

    def at(yx_to, z_to):
        return (dp, yx_to * NZ + z_to)

    core_peer = (z_hi * 2 + 1 - core, me)
    far_peer = ((1 - z_hi) * 2 + core, me)

    def remote(src, dst, sent, got, to):
        return pltpu.make_async_remote_copy(
            src_ref=src, dst_ref=dst, send_sem=sent, recv_sem=got, device_id=to, device_id_type=MESH
        )

    held_grads = slopes.at[pl.ds(0, pairs)]
    loads = [
        pltpu.make_async_copy(tokens, all_tokens.at[z], local_sem.at[4]),
        pltpu.make_async_copy(w_shard, state.at[0], local_sem.at[5]),
        pltpu.make_async_copy(m_shard, state.at[1], local_sem.at[6]),
        pltpu.make_async_copy(v_shard, state.at[2], local_sem.at[7]),
        pltpu.make_async_copy(residual, term, local_sem.at[8]),
        pltpu.make_async_copy(grads, held_grads, local_sem.at[9]),
    ]
    for load in loads:
        load.start()

    barrier = pltpu.get_barrier_semaphore()
    for d in range(1, 4):
        pl.semaphore_signal(barrier, inc=1, device_id=at(y * NX + lax.rem(x + d, NX), z), device_id_type=MESH)
        pl.semaphore_signal(barrier, inc=1, device_id=at(lax.rem(y + d, NY) * NX + x, z), device_id_type=MESH)
    for dz in range(1, NZ):
        pl.semaphore_signal(barrier, inc=1, device_id=at(yx, lax.rem(z + dz, NZ)), device_id_type=MESH)
    pl.semaphore_signal(barrier, inc=1, device_id=core_peer, device_id_type=MESH)
    pl.semaphore_signal(barrier, inc=1, device_id=far_peer, device_id_type=MESH)
    pl.semaphore_wait(barrier, 3 + 3 + NZ - 1 + 2)

    device_col = lax.broadcasted_iota(jnp.int32, (count, 1), 0)
    expert = lax.broadcasted_iota(jnp.int32, (count, count), 0) == lax.broadcasted_iota(jnp.int32, (count, count), 1)
    owner_col = jnp.sum(jnp.where(expert, owner_row[...], 0), axis=1, keepdims=True)
    before = (
        lax.broadcasted_iota(jnp.int32, (tok_rows, tok_rows), 0)
        < lax.broadcasted_iota(jnp.int32, (tok_rows, tok_rows), 1)
    ).astype(F32).astype(BF16)
    row_targets = [
        jnp.sum(jnp.where(device_col == routes_t[k : k + 1, :], owner_col, 0), axis=0, keepdims=True)
        for k in range(TOP)
    ]
    hits = [jnp.where(device_col == target, 1.0, 0.0) for target in row_targets]
    ranks = jnp.dot(sum(hits).astype(BF16), before, preferred_element_type=F32)
    target = jnp.concatenate(row_targets, axis=0)
    rank = jnp.concatenate([jnp.sum(hit * ranks, axis=0, keepdims=True) for hit in hits], axis=0)
    codes[z] = target * CAP + rank.astype(jnp.int32)
    loads[0].wait()

    def hop(source, up):
        step = 1 if up else -1
        to = at(yx, z + step)
        sems = (tok_up, code_up) if up else (tok_dn, code_dn)
        return (
            remote(all_tokens.at[source], all_tokens.at[source], sems[0].at[source], tok_got.at[source], to),
            remote(codes.at[source], codes.at[source], sems[1].at[source], code_got.at[source], to),
        )

    def send_hop(source):
        @pl.when((source <= z) & (z < NZ - 1))
        def _():
            for copy in hop(source, True):
                copy.start()

        @pl.when((source >= z) & (z > 0))
        def _():
            for copy in hop(source, False):
                copy.start()

    def wait_hop(source, up):
        for copy in hop(source, up):
            copy.wait_recv()

    send_hop(z)

    spread = (
        lax.broadcasted_iota(jnp.int32, (tok_rows, pairs), 0)
        == lax.broadcasted_iota(jnp.int32, (tok_rows, pairs), 1) // TOP
    ).astype(F32).astype(BF16)
    slot_of = lax.broadcasted_iota(jnp.int32, (TOP, pairs), 0) == lax.broadcasted_iota(jnp.int32, (TOP, pairs), 1) % TOP
    flat_target, flat_rank = [
        jnp.sum(
            jnp.where(slot_of, jnp.dot(v.astype(BF16), spread, preferred_element_type=F32), 0.0), axis=0, keepdims=True
        )
        for v in (target.astype(F32), rank)
    ]
    flat_codes = (flat_target * CAP + flat_rank).astype(jnp.int32)

    group = NX * NZ * CAP

    spot = (y, x, z)
    n_sems = len(route_sems())
    route_g = Route(
        spot, at, remote,
        lambda half, to: packed_g.at[to, :, pl.ds(2, 2)] if half else packed_g.at[:, to, pl.ds(0, 2)],
        lambda half, come: passed_g.at[half, come],
        lambda half, to: packed_g.at[y, to, pl.ds(2, 2)] if half else packed_g.at[to, x, pl.ds(0, 2)],
        lambda half, come, to: passed_g.at[half, come, to],
        lambda half, first, second: (
            relay_g.at[first, second, pl.ds(2, 2)] if half else relay_g.at[second, first, pl.ds(0, 2)]
        ),
        rest[:n_sems],
    )
    loads[5].wait()
    for y_to in range(NY):
        slot = lax.broadcasted_iota(jnp.int32, (group, pairs), 0) + y_to * group
        pick = jnp.where(slot == flat_codes, 1.0, 0.0).astype(BF16)
        got = jnp.dot(pick, held_grads[...], preferred_element_type=F32)
        for x_to in range(NX):
            for z_to in range(NZ):
                first = (x_to * NZ + z_to) * CAP
                packed_g[y_to, x_to, z_to] = got[first : first + CAP].astype(BF16)
    route_g.start()

    block = 2 * CAP

    wide = feats // 2

    def pair_route(pair, sems):
        def cols(half):
            return pl.ds(half * wide, wide)

        def rows_of(half, first, second):
            src = first * NX + second if half else second * NX + first
            return rows_x.at[pl.ds(pl.multiple_of((pair * PLANE + src) * block, 16), block), cols(half)]

        return Route(
            spot, at, remote,
            lambda half, to: (
                packed_x.at[pair, to, :, :, cols(half)] if half else packed_x.at[pair, :, to, :, cols(half)]
            ),
            lambda half, come: relay_x.at[pair, half, come],
            lambda half, to: (
                packed_x.at[pair, y, to, :, cols(half)] if half else packed_x.at[pair, to, x, :, cols(half)]
            ),
            lambda half, come, to: relay_x.at[pair, half, come, to],
            rows_of,
            sems,
        )

    def pack_pair(pair, route):
        part = NX * block
        s = lax.broadcasted_iota(jnp.int32, (part, tok_rows), 0)
        to = (s * 1366) >> 16
        half = (s * 2731) >> 16
        rank = s - half * CAP
        for y_to in range(NY):
            want = ((y_to * NX + to) * NZ + z) * CAP + rank
            picks = []
            for sub in range(2):
                source = codes[pair * 2 + sub]
                mine = jnp.where(half == 2 * to + sub, want, -1)
                hit = mine == source[0:1, :]
                for k in range(1, TOP):
                    hit = hit | (mine == source[k : k + 1, :])
                picks.append(jnp.where(hit, 1.0, 0.0).astype(BF16))
            pick = jnp.concatenate(picks, axis=1)
            for c in range(2):
                both = all_tokens[pl.ds(pair * 2, 2), :, pl.ds(c * wide, wide)].reshape(2 * tok_rows, wide)
                got = jnp.dot(pick, both, preferred_element_type=F32).astype(BF16)
                packed_x[pair, y_to, :, :, pl.ds(c * wide, wide)] = got.reshape(NX, block, wide)
        route.start()

    def take_hop(distance):
        @pl.when(z >= distance)
        def _():
            wait_hop(z - distance, True)
            send_hop(z - distance)

        @pl.when(z + distance < NZ)
        def _():
            wait_hop(z + distance, False)
            send_hop(z + distance)

    my_pair = z // 2
    route_mine = pair_route(my_pair, rest[n_sems : 2 * n_sems])
    route_other = pair_route(1 - my_pair, rest[2 * n_sems : 3 * n_sems])
    swaps = rest[3 * n_sems :]
    take_hop(1)
    pack_pair(my_pair, route_mine)
    take_hop(2)

    def w_rows(owner_dp):
        return w_full.at[pl.ds(pl.multiple_of(owner_dp * shard_rows, 16), shard_rows)]

    for load in loads[1:4]:
        load.wait()
    w_full[pl.ds(pl.multiple_of(dp * shard_rows, 16), shard_rows), :] = state[0]
    far_dp = (1 - z_hi) * 2 + core
    near_dp = z_hi * 2 + 1 - core
    w_far = remote(state.at[0], w_rows(dp), w_sent.at[0], w_got.at[0], far_peer)
    w_near = remote(state.at[0], w_rows(dp), w_sent.at[1], w_got.at[1], core_peer)
    w_pass = remote(w_rows(far_dp), w_rows(far_dp), w_sent.at[2], w_got.at[2], core_peer)
    w_far.start()
    w_near.start()

    route_g.relay_all()
    take_hop(3)
    pack_pair(1 - my_pair, route_other)
    route_mine.relay_all()

    pair = (moves[1, 1], moves[0, 1])
    half_swap = len(swaps) // 2
    swap_state = Swap(state, pair, (y, x, z), at, remote, swaps[:half_swap])
    swap_grad = Swap(grad_small, pair, (y, x, z), at, remote, swaps[half_swap:])

    route_g.wait_all()

    def g_line(z_to, z_from):
        return remote(relay_g.at[:, :, z_to], rows_g.at[z_from], gz_sent.at[z_to], gz_got.at[z_from], at(yx, z_to))

    for dz in range(1, NZ):
        g_line(lax.rem(z + dz, NZ), z).start()
    self_rows = pltpu.make_async_copy(relay_g.at[:, :, z], rows_g.at[z], local_sem.at[3])
    self_rows.start()
    route_other.relay_all()
    swap_state.start()

    w_far.wait_recv()
    w_pass.start()
    w_near.wait_recv()
    w_pass.wait_recv()

    def wait_line(z_from):
        remote(
            relay_g.at[:, :, z_from], rows_g.at[z_from], gz_sent.at[z_from], gz_got.at[z_from], at(yx, z_from)
        ).wait_recv()

    def forward(pair):
        per = PLANE // 2
        for part in range(2):
            base = pl.multiple_of((pair * PLANE + part * per) * block, 16)
            pre[pl.ds(0, per * block), :] = jnp.dot(
                rows_x[pl.ds(base, per * block), :], w_full[...], preferred_element_type=F32
            ) * scale

            def body(i, _):
                rows = pl.ds(pl.multiple_of(i * block, 16), block)
                src_y, src_x = part * (per // NX) + i // NX, i % NX
                g = jnp.concatenate(
                    [rows_g[pair * 2, src_y, src_x].astype(F32), rows_g[pair * 2 + 1, src_y, src_x].astype(F32)], axis=0
                )
                slope = (g * silu_slope(pre[rows, :])).astype(BF16)
                slopes[pl.ds(pl.multiple_of(base + i * block, 16), block), :] = slope
                return 0

            lax.fori_loop(0, per, body, 0)

    route_mine.wait_all()
    self_rows.wait()
    wait_line(my_pair * 4 + 1 - z)
    forward(my_pair)
    swap_state.second()
    route_other.wait_all()
    for sub in range(2):
        wait_line((1 - my_pair) * 2 + sub)
    forward(1 - my_pair)
    swap_state.along_z()

    tile = shard_rows // 2

    def gradient(shard):
        def body(i, _):
            first = pl.multiple_of(shard * shard_rows + i * tile, 128)
            part = lax.dot_general(
                rows_x[:, pl.ds(first, tile)], slopes[...], (((0,), (0,)), ((), ())),
                preferred_element_type=F32,
            )
            rows = pl.ds(pl.multiple_of(i * tile, 16), tile)
            term[shard, rows, :] = (part * scale + term[shard, rows, :].astype(F32)).astype(BF16)
            return 0

        lax.fori_loop(0, 2, body, 0)

    def to_core(z_hi_of):
        shard = z_hi_of * 2 + 1 - core
        return remote(term.at[shard], pair_got.at[z_hi_of], t_sent.at[z_hi_of], t_got.at[z_hi_of], core_peer)

    loads[4].wait()
    gradient(far_dp + 1 - 2 * core)
    to_core(1 - z_hi).start()
    gradient(far_dp)
    to_core(1 - z_hi).wait_recv()
    z_send[...] = (term[far_dp].astype(F32) + pair_got[1 - z_hi].astype(F32)).astype(BF16)
    z_copy = remote(z_send, z_got, t_sent.at[2], t_got.at[2], far_peer)
    z_copy.start()
    gradient(near_dp)
    to_core(z_hi).start()
    swap_state.fourth()
    gradient(dp)
    swap_state.last()
    to_core(z_hi).wait_recv()
    z_copy.wait_recv()
    grad_total = pre
    grad_total[pl.ds(0, shard_rows), :] = term[dp].astype(F32) + pair_got[z_hi].astype(F32) + z_got[...].astype(F32)
    grad_small[0] = grad_total[pl.ds(0, shard_rows), :].astype(BF16)

    swap_grad.start()
    swap_grad.second()
    swap_grad.along_z()
    swap_grad.fourth()
    swap_grad.last()
    swap_state.wait_last()
    swap_grad.wait_last()

    swap_state.wait_first()
    w_far.wait_send()
    w_near.wait_send()
    moved = (pair[0] == me) | (pair[1] == me)

    def update(i, _):
        rows = pl.ds(pl.multiple_of(i * 64, 16), 64)
        total = jnp.where(moved, swap_grad.got[0, rows, :].astype(F32), grad_total[rows, :])
        old = [
            jnp.where(moved, swap_state.got[c, rows, :].astype(F32), state[c, rows, :].astype(F32))
            for c in range(3)
        ]
        moment_one = beta_one * old[1] + (1.0 - beta_one) * total
        moment_two = beta_two * old[2] + (1.0 - beta_two) * total * total
        state[0, rows, :] = (old[0] - step_size * moment_one / (jnp.sqrt(moment_two) + epsilon)).astype(BF16)
        state[1, rows, :] = moment_one.astype(BF16)
        state[2, rows, :] = moment_two.astype(BF16)
        return 0

    lax.fori_loop(0, shard_rows // 64, update, 0)
    stores = [
        pltpu.make_async_copy(state.at[c], out, local_sem.at[5 + c]) for c, out in enumerate((w_out, m_out, v_out))
    ]
    for store in stores:
        store.start()

    for source in range(NZ):

        @pl.when((source <= z) & (z < NZ - 1))
        def _():
            for copy in hop(source, True):
                copy.wait_send()

        @pl.when((source >= z) & (z > 0))
        def _():
            for copy in hop(source, False):
                copy.wait_send()

    for route in (route_g, route_mine, route_other):
        route.wait_sent()
    for dz in range(1, NZ):
        g_line(lax.rem(z + dz, NZ), z).wait_send()
    w_pass.wait_send()
    to_core(0).wait_send()
    to_core(1).wait_send()
    z_copy.wait_send()
    swap_state.wait_sent()
    swap_grad.wait_first()
    swap_grad.wait_sent()
    for store in stores:
        store.wait()


def expert_update(tokens, routes, grads, owner, moves, w_shard, m_shard, v_shard, residual):
    tok_rows, feats = tokens.shape
    hidden = grads.shape[1]
    count = owner.shape[0]
    shard_rows = w_shard.shape[0]
    rows = count * CAP
    dma = pltpu.SemaphoreType.DMA
    vmem = pl.BlockSpec(memory_space=pltpu.VMEM)
    hbm = pl.BlockSpec(memory_space=pl.ANY)
    return pl.pallas_call(
        kernel,
        out_shape=[jax.ShapeDtypeStruct((shard_rows, hidden), BF16)] * 3,
        in_specs=[
            pl.BlockSpec(memory_space=pltpu.SMEM), vmem, vmem, hbm, hbm, hbm, hbm, hbm, hbm
        ],
        out_specs=[hbm] * 3,
        scratch_shapes=[
            pltpu.VMEM((NZ, TOP, tok_rows), jnp.int32),
            pltpu.VMEM((NZ, tok_rows, feats), BF16),
            pltpu.VMEM((2, NY, NX, 2 * CAP, feats), BF16),
            pltpu.VMEM((2, 2, 4, 4, 2 * CAP, feats // 2), BF16),
            pltpu.VMEM((rows, feats), BF16),
            pltpu.VMEM((NY, NX, NZ, CAP, hidden), BF16),
            pltpu.VMEM((2, 4, 4, 2, CAP, hidden), BF16),
            pltpu.VMEM((NY, NX, NZ, CAP, hidden), BF16),
            pltpu.VMEM((NZ, NY, NX, CAP, hidden), BF16),
            pltpu.VMEM((feats, hidden), BF16),
            pltpu.VMEM((max(rows // 4, shard_rows), hidden), F32),
            pltpu.VMEM((rows, hidden), BF16),
            pltpu.VMEM((4, shard_rows, hidden), BF16),
            pltpu.VMEM((2, shard_rows, hidden), BF16),
            pltpu.VMEM((shard_rows, hidden), BF16),
            pltpu.VMEM((shard_rows, hidden), BF16),
            dma((10,)),
            dma((NZ,)), dma((NZ,)), dma((NZ,)), dma((NZ,)), dma((NZ,)), dma((NZ,)),
            dma((NZ,)), dma((NZ,)),
            dma((3,)), dma((3,)), dma((3,)), dma((3,)),
            pltpu.VMEM((3, shard_rows, hidden), BF16),
            pltpu.VMEM((1, shard_rows, hidden), BF16),
            *route_sems(), *route_sems(), *route_sems(),
            *swap_scratch(3, shard_rows, hidden),
            *swap_scratch(1, shard_rows, hidden),
        ],
        compiler_params=pltpu.CompilerParams(
            collective_id=0, has_side_effects=True, vmem_limit_bytes=62 * 2**20
        ),
        name="expert_update",
    )(
        moves, routes.T, owner[None, :], tokens, grads, w_shard, m_shard, v_shard,
        residual.reshape(-1, shard_rows, hidden),
    )


def shards(tokens, routes, grad_act, owner, moves, weight, first_moment, second_moment, residual):
    hidden = grad_act.shape[2]
    new_w, new_m, new_v = expert_update(
        tokens, routes, grad_act.reshape(-1, hidden), owner, moves, weight[0], first_moment[0], second_moment[0],
        residual[0, 0],
    )
    return (new_w[None], new_m[None], new_v[None])


def solution(mesh):
    return jax.shard_map(
        shards,
        mesh=mesh,
        in_specs=(
            P(("dp", "expert"), None),
            P(("dp", "expert"), None),
            P(("dp", "expert"), None, None),
            P(),
            P(),
            P("expert", "dp", None),
            P("expert", "dp", None),
            P("expert", "dp", None),
            P("dp", "expert", None, None),
        ),
        out_specs=(P("expert", "dp", None), P("expert", "dp", None), P("expert", "dp", None)),
        check_vma=False,
    )
```

time: 278 us -> 232 us (0.83); the launches traced: 278 us -> 227 us
  Pallas kernels: 263 us -> 222 us
  other arithmetic: 4.58 us -> 0 us
  local copies, waits for them, and re-layouts: 9.34 us -> 5.08 us
    pallas_call x1, Pallas kernels: 263 us -> 222 us  [expert_update(): pl.pallas_call(kernel, out_shape=[jax.ShapeDtypeStruct((shard_rows, hidde...]
    unnamed x6 -> x5, local copies, waits for them, and re-layouts: 5.87 us -> 5.08 us
where the time goes in v2:
time: 232 us; the launch traced here: 227 us
  Pallas kernels  222 us (96%)
  local copies, waits for them, and re-layouts  5.08 us (2%)
    pallas_call x1, Pallas kernels, expert_update(): pl.pallas_call(kernel, out_shape=[jax.ShapeDtypeStruct((shard_rows, hidde...  222 us
    unnamed x5, local copies, waits for them, and re-layouts  5.08 us

profile of v2, /device:TPU:36, one launch (start us, length us, event | category | flops | bytes accessed | tf_op | source)
XLA Modules:
  0.0 227.3 jit_solution(6052466601783873119)
XLA Ops:
  0.6 221.5 %expert_update.1 = (bf16[512,768]{1,0:T(8,128)(2,1)}, bf16[512,768]{1,0:T(8,128)(2,1)}, bf16[512,768]{1,0:T(8,128)(2,1)}) custom-call(s32[2,2]{1,0:T(2,128)} %moves.1, s32[8,128]{1,0:T(8,128)} %bitcast.18, s32[1,64]{1,0:T(1,128)} %bitcast.19, bf16[128,2048]{1,0:T(8,128)(2,1)} %tokens.1, bf16[1024,768]{1,0:T(8,128)(2,1)} %bitcast.11, ...), custom_call_target="tpu_custom_call" | custom-call | tf_op jit(solution)/shard_map/expert_update/pallas_call | solution.py:645
  222.2 0.0 copy-start
  222.2 2.1 copy.15
  224.3 2.1 copy.16
  226.4 0.0 copy-done
  226.4 0.9 copy.17
Async XLA Ops:
  222.2 4.2 %copy-start = (bf16[512,768]{1,0:T(8,128)(2,1)S(1)}, bf16[512,768]{1,0:T(8,128)(2,1)}, u32[]{:S(2)}) copy-start(bf16[512,768]{1,0:T(8,128)(2,1)} %get-tuple-element.8) | copy-start | bytes 2359300

commit v3 on v2

--- a/solution.py
+++ b/solution.py
@@ -256,7 +256,7 @@
     w_out, m_out, v_out,
     codes, all_tokens, packed_x, relay_x, rows_x, packed_g, passed_g, relay_g, rows_g, w_full, pre, slopes,
     term, pair_got, z_send, z_got,
-    local_sem, tok_up, tok_dn, tok_got, code_up, code_dn, code_got,
+    local_sem, tok_sent, tok_got, code_sent, code_got,
     gz_sent, gz_got, w_sent, w_got, t_sent, t_got,
     state, grad_small, *rest,
 ):
@@ -275,6 +275,12 @@
 
     def at(yx_to, z_to):
         return (dp, yx_to * NZ + z_to)
+
+    turn = 1 - 2 * core
+
+    def ring(step):
+        p = lax.rem(z_hi * NZ + z + step + 2 * NZ, 2 * NZ)
+        return ((p // NZ) * 2 + core, yx * NZ + p % NZ), p % NZ
 
     core_peer = (z_hi * 2 + 1 - core, me)
     far_peer = ((1 - z_hi) * 2 + core, me)
@@ -302,9 +308,11 @@
         pl.semaphore_signal(barrier, inc=1, device_id=at(lax.rem(y + d, NY) * NX + x, z), device_id_type=MESH)
     for dz in range(1, NZ):
         pl.semaphore_signal(barrier, inc=1, device_id=at(yx, lax.rem(z + dz, NZ)), device_id_type=MESH)
+    for step in (1, -1, 2, -2):
+        pl.semaphore_signal(barrier, inc=1, device_id=ring(step)[0], device_id_type=MESH)
     pl.semaphore_signal(barrier, inc=1, device_id=core_peer, device_id_type=MESH)
     pl.semaphore_signal(barrier, inc=1, device_id=far_peer, device_id_type=MESH)
-    pl.semaphore_wait(barrier, 3 + 3 + NZ - 1 + 2)
+    pl.semaphore_wait(barrier, 3 + 3 + NZ - 1 + 4 + 2)
 
     device_col = lax.broadcasted_iota(jnp.int32, (count, 1), 0)
     expert = lax.broadcasted_iota(jnp.int32, (count, count), 0) == lax.broadcasted_iota(jnp.int32, (count, count), 1)
@@ -324,31 +332,33 @@
     codes[z] = target * CAP + rank.astype(jnp.int32)
     loads[0].wait()
 
-    def hop(source, up):
-        step = 1 if up else -1
-        to = at(yx, z + step)
-        sems = (tok_up, code_up) if up else (tok_dn, code_dn)
+    def hop(source, step, sent):
+        to = ring(step)[0]
         return (
-            remote(all_tokens.at[source], all_tokens.at[source], sems[0].at[source], tok_got.at[source], to),
-            remote(codes.at[source], codes.at[source], sems[1].at[source], code_got.at[source], to),
+            remote(all_tokens.at[source], all_tokens.at[source], tok_sent.at[sent], tok_got.at[source], to),
+            remote(codes.at[source], codes.at[source], code_sent.at[sent], code_got.at[source], to),
         )
 
-    def send_hop(source):
-        @pl.when((source <= z) & (z < NZ - 1))
-        def _():
-            for copy in hop(source, True):
-                copy.start()
-
-        @pl.when((source >= z) & (z > 0))
-        def _():
-            for copy in hop(source, False):
-                copy.start()
-
-    def wait_hop(source, up):
-        for copy in hop(source, up):
+    behind = ring(-turn)[1]
+    hops = hop(z, turn, 0) + hop(z, -turn, 1)
+    passed_hop = hop(behind, turn, 2)
+
+    def wait_hop(source):
+        for copy in hop(source, 1, 0):
             copy.wait_recv()
 
-    send_hop(z)
+    for copy in hops:
+        copy.start()
+
+    for load in loads[1:4]:
+        load.wait()
+    pair = (moves[1, 1], moves[0, 1])
+    swaps = rest[3 * len(route_sems()) :]
+    half_swap = len(swaps) // 2
+    swap_state = Swap(state, pair, (y, x, z), at, remote, swaps[:half_swap])
+    swap_grad = Swap(grad_small, pair, (y, x, z), at, remote, swaps[half_swap:])
+
+    swap_state.start()
 
     spread = (
         lax.broadcasted_iota(jnp.int32, (tok_rows, pairs), 0)
@@ -438,30 +448,19 @@
                 packed_x[pair, y_to, :, :, pl.ds(c * wide, wide)] = got.reshape(NX, block, wide)
         route.start()
 
-    def take_hop(distance):
-        @pl.when(z >= distance)
-        def _():
-            wait_hop(z - distance, True)
-            send_hop(z - distance)
-
-        @pl.when(z + distance < NZ)
-        def _():
-            wait_hop(z + distance, False)
-            send_hop(z + distance)
-
     my_pair = z // 2
     route_mine = pair_route(my_pair, rest[n_sems : 2 * n_sems])
     route_other = pair_route(1 - my_pair, rest[2 * n_sems : 3 * n_sems])
-    swaps = rest[3 * n_sems :]
-    take_hop(1)
+    wait_hop(behind)
+    for copy in passed_hop:
+        copy.start()
+    wait_hop(ring(turn)[1])
     pack_pair(my_pair, route_mine)
-    take_hop(2)
+    swap_state.second()
 
     def w_rows(owner_dp):
         return w_full.at[pl.ds(pl.multiple_of(owner_dp * shard_rows, 16), shard_rows)]
 
-    for load in loads[1:4]:
-        load.wait()
     w_full[pl.ds(pl.multiple_of(dp * shard_rows, 16), shard_rows), :] = state[0]
     far_dp = (1 - z_hi) * 2 + core
     near_dp = z_hi * 2 + 1 - core
@@ -472,26 +471,24 @@
     w_near.start()
 
     route_g.relay_all()
-    take_hop(3)
+    wait_hop(ring(2 * turn)[1])
     pack_pair(1 - my_pair, route_other)
+    swap_state.along_z()
     route_mine.relay_all()
 
-    pair = (moves[1, 1], moves[0, 1])
-    half_swap = len(swaps) // 2
-    swap_state = Swap(state, pair, (y, x, z), at, remote, swaps[:half_swap])
-    swap_grad = Swap(grad_small, pair, (y, x, z), at, remote, swaps[half_swap:])
-
     route_g.wait_all()
 
-    def g_line(z_to, z_from):
-        return remote(relay_g.at[:, :, z_to], rows_g.at[z_from], gz_sent.at[z_to], gz_got.at[z_from], at(yx, z_to))
-
-    for dz in range(1, NZ):
-        g_line(lax.rem(z + dz, NZ), z).start()
+    def g_line(step):
+        device, z_to = ring(step)
+        return remote(relay_g.at[:, :, z_to], rows_g.at[z], gz_sent.at[z_to], gz_got.at[z], device)
+
+    g_lines = [g_line(2 * turn), g_line(turn), g_line(-turn)]
+    for copy in g_lines:
+        copy.start()
     self_rows = pltpu.make_async_copy(relay_g.at[:, :, z], rows_g.at[z], local_sem.at[3])
     self_rows.start()
     route_other.relay_all()
-    swap_state.start()
+    swap_state.fourth()
 
     w_far.wait_recv()
     w_pass.start()
@@ -527,12 +524,11 @@
     self_rows.wait()
     wait_line(my_pair * 4 + 1 - z)
     forward(my_pair)
-    swap_state.second()
     route_other.wait_all()
     for sub in range(2):
         wait_line((1 - my_pair) * 2 + sub)
     forward(1 - my_pair)
-    swap_state.along_z()
+    swap_state.last()
 
     tile = shard_rows // 2
 
@@ -563,9 +559,7 @@
     z_copy.start()
     gradient(near_dp)
     to_core(z_hi).start()
-    swap_state.fourth()
     gradient(dp)
-    swap_state.last()
     to_core(z_hi).wait_recv()
     z_copy.wait_recv()
     grad_total = pre
@@ -606,22 +600,10 @@
     for store in stores:
         store.start()
 
-    for source in range(NZ):
-
-        @pl.when((source <= z) & (z < NZ - 1))
-        def _():
-            for copy in hop(source, True):
-                copy.wait_send()
-
-        @pl.when((source >= z) & (z > 0))
-        def _():
-            for copy in hop(source, False):
-                copy.wait_send()
-
+    for copy in hops + passed_hop + tuple(g_lines):
+        copy.wait_send()
     for route in (route_g, route_mine, route_other):
         route.wait_sent()
-    for dz in range(1, NZ):
-        g_line(lax.rem(z + dz, NZ), z).wait_send()
     w_pass.wait_send()
     to_core(0).wait_send()
     to_core(1).wait_send()
@@ -667,7 +649,7 @@
             pltpu.VMEM((shard_rows, hidden), BF16),
             pltpu.VMEM((shard_rows, hidden), BF16),
             dma((10,)),
-            dma((NZ,)), dma((NZ,)), dma((NZ,)), dma((NZ,)), dma((NZ,)), dma((NZ,)),
+            dma((3,)), dma((NZ,)), dma((3,)), dma((NZ,)),
             dma((NZ,)), dma((NZ,)),
             dma((3,)), dma((3,)), dma((3,)), dma((3,)),
             pltpu.VMEM((3, shard_rows, hidden), BF16),

time: 232 us -> 206 us (0.89)
  Pallas kernels: 222 us -> 197 us
    pallas_call x1, Pallas kernels: 222 us -> 197 us  [expert_update(): pl.pallas_call(kernel, out_shape=[jax.ShapeDtypeStruct((shard_rows, hidde...]
where the time goes in v3:
time: 206 us; the launch traced here: 203 us
  Pallas kernels  197 us (96%)
  local copies, waits for them, and re-layouts  5.08 us (2%)
    pallas_call x1, Pallas kernels, expert_update(): pl.pallas_call(kernel, out_shape=[jax.ShapeDtypeStruct((shard_rows, hidde...  197 us
    unnamed x5, local copies, waits for them, and re-layouts  5.08 us

profile of v3, /device:TPU:36, one launch (start us, length us, event | category | flops | bytes accessed | tf_op | source)
XLA Modules:
  0.0 203.2 jit_solution(9076446197347458899)
XLA Ops:
  0.6 197.5 %expert_update.1 = (bf16[512,768]{1,0:T(8,128)(2,1)}, bf16[512,768]{1,0:T(8,128)(2,1)}, bf16[512,768]{1,0:T(8,128)(2,1)}) custom-call(s32[2,2]{1,0:T(2,128)} %moves.1, s32[8,128]{1,0:T(8,128)} %bitcast.18, s32[1,64]{1,0:T(1,128)} %bitcast.19, bf16[128,2048]{1,0:T(8,128)(2,1)} %tokens.1, bf16[1024,768]{1,0:T(8,128)(2,1)} %bitcast.11, ...), custom_call_target="tpu_custom_call" | custom-call | tf_op jit(solution)/shard_map/expert_update/pallas_call | solution.py:627
  198.1 0.0 copy-start
  198.1 2.1 %copy.15 = bf16[1,512,768]{2,1,0:T(8,128)(2,1)} copy(bf16[1,512,768]{2,1,0:T(8,128)(2,1)} %bitcast.17) | data formatting | bytes 1572864
  200.3 2.1 %copy.16 = bf16[1,512,768]{2,1,0:T(8,128)(2,1)} copy(bf16[1,512,768]{2,1,0:T(8,128)(2,1)} %bitcast.16) | data formatting | bytes 1572864
  202.3 0.0 copy-done
  202.3 0.9 copy.17
Async XLA Ops:
  198.1 4.2 %copy-start = (bf16[512,768]{1,0:T(8,128)(2,1)S(1)}, bf16[512,768]{1,0:T(8,128)(2,1)}, u32[]{:S(2)}) copy-start(bf16[512,768]{1,0:T(8,128)(2,1)} %get-tuple-element.8) | copy-start | bytes 2359300

commit v4 on v3

--- a/solution.py
+++ b/solution.py
@@ -668,13 +668,28 @@
     )
 
 
+def hand_over(w_in, m_in, v_in, w_out, m_out, v_out):
+    w_out[...] = w_in[...]
+    m_out[...] = m_in[...]
+    v_out[...] = v_in[...]
+
+
 def shards(tokens, routes, grad_act, owner, moves, weight, first_moment, second_moment, residual):
     hidden = grad_act.shape[2]
     new_w, new_m, new_v = expert_update(
         tokens, routes, grad_act.reshape(-1, hidden), owner, moves, weight[0], first_moment[0], second_moment[0],
         residual[0, 0],
     )
-    return (new_w[None], new_m[None], new_v[None])
+    news = (new_w[None], new_m[None], new_v[None])
+    part = pl.BlockSpec((1, new_w.shape[0] // 4, hidden), lambda i: (0, i, 0))
+    return pl.pallas_call(
+        hand_over,
+        grid=(4,),
+        out_shape=[jax.ShapeDtypeStruct(new.shape, new.dtype) for new in news],
+        in_specs=[part] * 3,
+        out_specs=[part] * 3,
+        name="finish",
+    )(*news)
 
 
 def solution(mesh):

time: 206 us -> 204 us (level)
  local copies, waits for them, and re-layouts: 5.08 us -> 0 us
  Pallas kernels: 197 us -> 201 us
    unnamed x5 -> x0, local copies, waits for them, and re-layouts: 5.08 us -> none
    pallas_call x0 -> x1, Pallas kernels: none -> 3.91 us  [shards(): pl.pallas_call(hand_over, grid=(4,), out_shape=[jax.ShapeDtypeStruct(new....]
where the time goes in v4:
time: 204 us; the launch traced here: 202 us
  Pallas kernels  201 us (99%)
    pallas_call x1, Pallas kernels, expert_update(): pl.pallas_call(kernel, out_shape=[jax.ShapeDtypeStruct((shard_rows, hidde...  198 us

profile of v4, /device:TPU:36, one launch (start us, length us, event | category | flops | bytes accessed | tf_op | source)
XLA Modules:
  0.0 202.1 jit_solution(14838871157911690786)
XLA Ops:
  0.6 197.5 %expert_update.1 = (bf16[512,768]{1,0:T(8,128)(2,1)}, bf16[512,768]{1,0:T(8,128)(2,1)}, bf16[512,768]{1,0:T(8,128)(2,1)}) custom-call(s32[2,2]{1,0:T(2,128)} %moves.1, s32[8,128]{1,0:T(8,128)} %bitcast.18, s32[1,64]{1,0:T(1,128)} %bitcast.19, bf16[128,2048]{1,0:T(8,128)(2,1)} %tokens.1, bf16[1024,768]{1,0:T(8,128)(2,1)} %bitcast.11, ...), custom_call_target="tpu_custom_call" | custom-call | tf_op jit(solution)/shard_map/expert_update/pallas_call | solution.py:627
  198.2 3.9 %finish.1 = (bf16[1,512,768]{2,1,0:T(8,128)(2,1)}, bf16[1,512,768]{2,1,0:T(8,128)(2,1)}, bf16[1,512,768]{2,1,0:T(8,128)(2,1)}) custom-call(bf16[1,512,768]{2,1,0:T(8,128)(2,1)} %bitcast.15, bf16[1,512,768]{2,1,0:T(8,128)(2,1)} %bitcast.16, bf16[1,512,768]{2,1,0:T(8,128)(2,1)} %bitcast.17), custom_call_target="tpu_custom_call" | custom-call | tf_op jit(solution)/shard_map/finish/pallas_call | solution.py:685
